TPU v7x, 512 devices: a whole 4x8x8 slice. The times are simulated.
512 devices in a mesh: dp: 16 (over y_lo, x), ctx: 32 (over z, y_hi, core).
Axes of the slice: x: 4, y: 8 (y_hi: 2, y_lo: 4; y = y_hi * 4 + y_lo), z: 8, core: 2. Of those that a mesh axis runs over, the one named last changes fastest.
Arguments:
- tokens: bfloat16 [65536, 1024], P(('dp', 'ctx')), may hold values from -6 to 6
- grad_out: bfloat16 [65536, 1024], P(('dp', 'ctx')), may hold values from -6 to 6
- gates: bfloat16 [65536, 8], P(('dp', 'ctx')), may hold values from 0.049804688 to 0.5
- expert_ids: int32 [65536, 8], P(('dp', 'ctx')), may hold values from 0 to 63, all different within a row; in each aligned block of 128 rows (0 to 127, 128 to 255, ...) at most 18 rows name the same one
- w_up: bfloat16 [64, 1024, 384], P('ctx', 'dp'), may hold values from -0.1875 to 0.1875
- w_down: bfloat16 [64, 384, 1024], P('ctx', None, 'dp'), may hold values from -0.3125 to 0.3125
Outputs:
- grad_tokens: bfloat16 [65536, 1024], P(('dp', 'ctx'))
- grad_gates: bfloat16 [65536, 8], P(('dp', 'ctx'))
- grad_up: bfloat16 [64, 1024, 384], P('ctx', 'dp')
- grad_down: bfloat16 [64, 384, 1024], P('ctx', None, 'dp')
Inputs may be any that keep to these rules, and one draw needn't show every extreme that they name: `expert_ids`: each row names 8 different experts. Among the 128 rows of one device no expert is named more than 18 times, and in every draw some expert is named exactly 18 times in some device's rows.
All inputs are finite; a program needn't handle non-finite values.
Results may differ from a plain program's by a relative error of at most 0.023.
Values may be sent and summed in bfloat16 or wider, within the bound.
No kernel may reach another device: no remote copies, remote signals or barrier semaphores. Data moves between devices by JAX's collectives and lax.ppermute only.
A program may use at most 64 MiB of HBM per device.

v0:
```python
import jax
import jax.numpy as jnp
from jax import lax
from jax.sharding import PartitionSpec as P


def swish_grad(pre_act, sigmoid_a):
    return sigmoid_a * (1.0 + pre_act * (1.0 - sigmoid_a))


def per_device(tokens, grad_out, gates, expert_ids, w_up, w_down):
    tok_rows, width = tokens.shape
    top_count = expert_ids.shape[1]
    ctx_count = lax.axis_size("ctx")
    exp_local = w_up.shape[0]
    experts_all = exp_local * ctx_count
    capacity = tok_rows * top_count * 9 // (8 * experts_all)
    flat_ids = expert_ids.reshape(-1)
    onehot = (flat_ids[:, None] == jnp.arange(experts_all, dtype=jnp.int32)[None, :]).astype(
        jnp.int32
    )
    earlier = jnp.cumsum(onehot, axis=0) - onehot
    slot_pos = jnp.sum(earlier * onehot, axis=1)
    owner = flat_ids // exp_local
    local_idx = flat_ids % exp_local
    target = (local_idx * ctx_count + owner) * capacity + slot_pos
    token_pos = jnp.arange(tok_rows * top_count, dtype=jnp.int32) // top_count
    buffer_len = experts_all * capacity
    source_row = jnp.full((buffer_len,), tok_rows, jnp.int32).at[target].set(token_pos)
    paired = jnp.concatenate((tokens, grad_out), axis=1)
    send_pair = jnp.take(paired, source_row, axis=0, mode="fill", fill_value=0)
    send_gate = jnp.zeros((buffer_len,), jnp.bfloat16).at[target].set(gates.reshape(-1))
    block_shape = (exp_local, ctx_count, capacity, width)
    slot_shape = (exp_local, ctx_count, capacity)
    recv_pair, recv_gate = (
        lax.all_to_all(
            send_pair.reshape(exp_local, ctx_count, capacity, 2 * width),
            "ctx",
            split_axis=1,
            concat_axis=1,
            tiled=True,
        ),
        lax.all_to_all(
            send_gate.reshape(slot_shape), "ctx", split_axis=1, concat_axis=1, tiled=True
        ),
    )
    row_len = ctx_count * capacity
    rows_pair = recv_pair.reshape(exp_local, row_len, 2 * width)
    rows_x = rows_pair[:, :, :width]
    rows_grad = rows_pair[:, :, width:]
    rows_gate = recv_gate.reshape(exp_local, row_len)
    up_full, down_full = (
        lax.all_gather(w_up, "dp", axis=1, tiled=True),
        lax.all_gather(w_down, "dp", axis=2, tiled=True),
    )
    pre_act = jnp.einsum("erd,edf->erf", rows_x, up_full, preferred_element_type=jnp.float32)
    sigmoid_a = jax.nn.sigmoid(pre_act)
    hidden = (pre_act * sigmoid_a).astype(jnp.bfloat16)
    outputs = jnp.einsum(
        "erf,efd->erd", hidden, down_full, preferred_element_type=jnp.float32
    ).astype(jnp.bfloat16)
    grad_y = (rows_gate[:, :, None].astype(jnp.float32) * rows_grad).astype(jnp.bfloat16)
    grad_h = jnp.einsum("erd,efd->erf", grad_y, down_full, preferred_element_type=jnp.float32)
    grad_a = (grad_h * swish_grad(pre_act, sigmoid_a)).astype(jnp.bfloat16)
    grad_rows = jnp.einsum(
        "erf,edf->erd", grad_a, up_full, preferred_element_type=jnp.float32
    ).astype(jnp.bfloat16)
    back_rows = lax.all_to_all(
        grad_rows.reshape(block_shape), "ctx", split_axis=1, concat_axis=1, tiled=True
    )
    back_out = lax.all_to_all(
        outputs.reshape(block_shape), "ctx", split_axis=1, concat_axis=1, tiled=True
    )
    picked_out = back_out.reshape(-1, width)[target].reshape(tok_rows, top_count, width)
    picked_scores = jnp.einsum(
        "td,tkd->tk", grad_out, picked_out, preferred_element_type=jnp.float32
    ).astype(jnp.bfloat16)
    picked_rows = back_rows.reshape(-1, width)[target].reshape(tok_rows, top_count, width)
    grad_tokens = jnp.sum(picked_rows.astype(jnp.float32), axis=1).astype(jnp.bfloat16)
    grad_tokens, grad_gates = (grad_tokens, picked_scores)
    up_part = jnp.einsum("erc,erf->cef", rows_x, grad_a, preferred_element_type=jnp.float32)
    down_part = jnp.einsum("erf,erc->cef", hidden, grad_y, preferred_element_type=jnp.float32)
    summed = lax.psum_scatter(
        jnp.stack((up_part, down_part), axis=1).astype(jnp.bfloat16),
        "dp",
        scatter_dimension=0,
        tiled=True,
    ).astype(jnp.float32)
    grad_up = jnp.transpose(summed[:, 0], (1, 0, 2)).astype(jnp.bfloat16)
    grad_down = jnp.transpose(summed[:, 1], (1, 2, 0)).astype(jnp.bfloat16)
    grad_up, grad_down = (grad_up, grad_down)
    return (grad_tokens, grad_gates, grad_up, grad_down)


def solution(mesh):
    in_specs = (
        P(("dp", "ctx"), None),
        P(("dp", "ctx"), None),
        P(("dp", "ctx"), None),
        P(("dp", "ctx"), None),
        P("ctx", "dp", None),
        P("ctx", None, "dp"),
    )
    out_specs = (
        P(("dp", "ctx"), None),
        P(("dp", "ctx"), None),
        P("ctx", "dp", None),
        P("ctx", None, "dp"),
    )
    return jax.shard_map(
        per_device, mesh=mesh, in_specs=in_specs, out_specs=out_specs, check_vma=False
    )
```

profile of v0, /device:TPU:64, one launch (start us, length us, event | category | flops | bytes accessed | tf_op | source)
XLA Modules:
  0.0 740.7 jit_solution(15632867575689190050)
XLA Ops:
  7.2 0.8 copy.52
  8.3 18.0 %reduce-window.6 = s32[64,8,128]{2,1,0:T(8,128)S(1)} reduce-window(s32[64,8,128]{2,1,0:T(8,128)S(1)} %fusion.20, s32[]{:T(128)} %constant.60.clone.1), window={size=1x1x128 pad=0_0x0_0x127_0}, to_apply=%region_0.0 | reduce-window | flops 8323072 | bytes 524292 | tf_op jit(solution)/shard_map/reduce-window
  27.3 7.6 %scatter_custom_fusion = bf16[1152]{0:T(1024)(128)(2,1)S(1)} fusion(s32[1024]{0:T(1024)S(1)} %bitcast.59, bf16[1024]{0:T(1024)(128)(2,1)S(1)} %reshape.238, bf16[]{:T(256)} %constant.59.clone.1), kind=kCustom, calls=%fused_computation.60 | custom fusion | bytes 2306 | tf_op jit(solution)/shard_map/scatter | solution.py:32
  34.9 0.1 reshape.201
  35.0 0.6 copy.58
  35.6 15.4 %all-to-all-start = ((bf16[2,32,18]{2,0,1:T(2,128)(2,1)}), bf16[2,32,18]{2,0,1:T(2,128)(2,1)S(1)}, u32[]{:S(2)}, u32[]{:S(2)}) async-start(bf16[2,32,18]{2,0,1:T(2,128)(2,1)} %copy.58), calls=%async_computation | async-start | bytes 32768 | tf_op jit(solution)/shard_map/all_to_all | solution.py:43
  51.0 4.8 scatter_custom_fusion.1
  55.9 6.0 gather_fusion
  62.0 7.5 %gather.13 = bf16[2,32,18,2048]{3,2,1,0:T(8,128)(2,1)} reshape(bf16[1152,2048]{1,0:T(8,128)(2,1)} %gather_fusion) | data formatting | bytes 9437184 | tf_op jit(solution)/shard_map/jit(_take)/gather | solution.py:31
  69.5 0.1 broadcast_in_dim.27
  69.6 6.0 broadcast_select_fusion
  75.6 9.9 %copy.61 = bf16[2,32,18,2048]{3,0,2,1:T(2,128)(2,1)} copy(bf16[2,32,18,2048]{3,2,1,0:T(8,128)(2,1)} %broadcast_select_fusion) | data formatting | bytes 9437184 | tf_op jit(solution)/shard_map/jit(_take)/select_n | solution.py:31
  85.5 12.2 %all-to-all-start.1 = ((bf16[2,32,18,2048]{3,0,2,1:T(2,128)(2,1)}), bf16[2,32,18,2048]{3,0,2,1:T(2,128)(2,1)}, u32[]{:S(2)}, u32[]{:S(2)}) async-start(bf16[2,32,18,2048]{3,0,2,1:T(2,128)(2,1)} %copy.61), calls=%async_computation.1 | async-start | bytes 9437184 | tf_op jit(solution)/shard_map/all_to_all | solution.py:36
  97.8 0.7 all-gather.5.cloned.1.call-update
  98.5 0.2 all-gather.3.cloned.1.call-start
  98.7 0.5 all-gather.3.cloned.1.call-update
  99.6 142.2 %all-to-all-done.1 = bf16[2,32,18,2048]{3,0,2,1:T(2,128)(2,1)} async-done(((bf16[2,32,18,2048]{3,0,2,1:T(2,128)(2,1)}), bf16[2,32,18,2048]{3,0,2,1:T(2,128)(2,1)}, u32[]{:S(2)}, u32[]{:S(2)}) %all-to-all-start.1) | async-done | bytes 4718624 | tf_op jit(solution)/shard_map/all_to_all | solution.py:36
  241.7 7.1 fusion.30
  248.9 32.6 %all-gather.5.cloned.1.call-done = bf16[2,1024,384]{2,1,0:T(8,128)(2,1)} async-done(((bf16[2,64,384]{2,1,0:T(8,128)(2,1)}), bf16[2,1024,384]{2,1,0:T(8,128)(2,1)}) %all-gather.5.cloned.1.call-update) | async-done | bytes 1572880 | tf_op jit(solution)/shard_map/all_gather | solution.py:53
  281.5 4.7 fusion.4
  286.2 99.7 %all-gather.3.cloned.1.call-done = bf16[2,384,1024]{1,2,0:T(8,128)(2,1)} async-done(((bf16[2,384,64]{1,2,0:T(8,128)(2,1)}), bf16[2,384,1024]{1,2,0:T(8,128)(2,1)}) %all-gather.3.cloned.1.call-update) | async-done | bytes 1572880 | tf_op jit(solution)/shard_map/all_gather | solution.py:54
  385.9 3.9 multiply_convert_fusion.4
  389.8 1.4 convolution_convert_fusion.1
  391.3 3.9 copy.64
  395.2 12.6 %all-to-all-start.2 = ((bf16[2,32,18,1024]{3,0,2,1:T(2,128)(2,1)}), bf16[2,32,18,1024]{3,0,2,1:T(2,128)(2,1)S(1)}, u32[]{:S(2)}, u32[]{:S(2)}) async-start(bf16[2,32,18,1024]{3,0,2,1:T(2,128)(2,1)} %bitcast.5), calls=%async_computation.2 | async-start | bytes 4718592 | tf_op jit(solution)/shard_map/all_to_all | solution.py:68
  407.8 3.4 convolution_convert_fusion
  411.2 3.9 copy.66
  415.1 52.4 %all-to-all-done.2 = bf16[2,32,18,1024]{3,0,2,1:T(2,128)(2,1)S(1)} async-done(((bf16[2,32,18,1024]{3,0,2,1:T(2,128)(2,1)}), bf16[2,32,18,1024]{3,0,2,1:T(2,128)(2,1)S(1)}, u32[]{:S(2)}, u32[]{:S(2)}) %all-to-all-start.2) | async-done | bytes 2359328 | tf_op jit(solution)/shard_map/all_to_all | solution.py:68
  467.5 1.4 copy-done
  468.8 18.3 %all-to-all-start.3 = ((bf16[2,32,18,1024]{3,0,2,1:T(2,128)(2,1)}), bf16[2,32,18,1024]{3,0,2,1:T(2,128)(2,1)}, u32[]{:S(2)}, u32[]{:S(2)}) async-start(bf16[2,32,18,1024]{3,0,2,1:T(2,128)(2,1)} %bitcast.7), calls=%async_computation.3 | async-start | bytes 4718592 | tf_op jit(solution)/shard_map/all_to_all | solution.py:71
  487.2 3.4 fusion.12
  490.6 1.8 fusion.15
  492.4 0.3 pad_maximum_fusion
  492.7 5.9 copy.69
  498.7 1.4 dynamic-slice
  500.7 200.3 %all-reduce.3.cloned.1.call-done = bf16[1024,2,2,384]{3,2,1,0:T(2,128)(2,1)} async-done(((bf16[1024,2,2,384]{3,2,1,0:T(2,128)(2,1)}), bf16[1024,2,2,384]{3,2,1,0:T(2,128)(2,1)}) %all-reduce.3.cloned.1.call-update) | async-done | bytes 3145744
  701.0 1.1 dynamic-slice_bitcast_fusion
  702.1 0.7 copy.70
  702.8 0.7 copy.71
  703.4 2.5 copy.65
  705.9 2.9 reshape.204
  708.9 5.4 gather_fusion.1
  714.2 3.7 bitcast_reduce_fusion
  718.0 4.2 copy.67
  722.1 2.9 reshape.207
  725.1 5.4 gather_fusion.2
  730.4 2.8 fusion
  733.3 0.7 copy.73
  (45 shorter events, 1.7 us)
Async XLA Ops:
  7.2 19.7 %copy-start.7 = (bf16[128,8]{0,1:T(8,128)(2,1)S(1)}, bf16[128,8]{0,1:T(8,128)(2,1)}, u32[]{:S(2)}) copy-start(bf16[128,8]{0,1:T(8,128)(2,1)} %param.8) | copy-start | bytes 6148
  7.2 48.7 %copy-start.5 = (bf16[128,1024]{1,0:T(8,128)(2,1)S(1)}, bf16[128,1024]{1,0:T(8,128)(2,1)}, u32[]{:S(2)}) copy-start(bf16[128,1024]{1,0:T(8,128)(2,1)} %param.6) | copy-start | bytes 786436
  7.2 48.7 %copy-start.6 = (bf16[128,1024]{1,0:T(8,128)(2,1)S(1)}, bf16[128,1024]{1,0:T(8,128)(2,1)}, u32[]{:S(2)}) copy-start(bf16[128,1024]{1,0:T(8,128)(2,1)} %param.7) | copy-start | bytes 786436
  35.6 49.9 %all-to-all-start = ((bf16[2,32,18]{2,0,1:T(2,128)(2,1)}), bf16[2,32,18]{2,0,1:T(2,128)(2,1)S(1)}, u32[]{:S(2)}, u32[]{:S(2)}) async-start(bf16[2,32,18]{2,0,1:T(2,128)(2,1)} %copy.58), calls=%async_computation | async-start | bytes 32768 | tf_op jit(solution)/shard_map/all_to_all | solution.py:43
  85.5 156.2 %all-to-all-start.1 = ((bf16[2,32,18,2048]{3,0,2,1:T(2,128)(2,1)}), bf16[2,32,18,2048]{3,0,2,1:T(2,128)(2,1)}, u32[]{:S(2)}, u32[]{:S(2)}) async-start(bf16[2,32,18,2048]{3,0,2,1:T(2,128)(2,1)} %copy.61), calls=%async_computation.1 | async-start | bytes 9437184 | tf_op jit(solution)/shard_map/all_to_all | solution.py:36
  97.8 183.7 %all-gather.5.cloned.1.call-start = ((), (), s32[]{:S(2)}) async-start(), calls=%async_computation.5 | async-start | bytes 1671168 | tf_op jit(solution)/shard_map/all_gather | solution.py:53
  98.5 287.4 %all-gather.3.cloned.1.call-start = ((), (), s32[]{:S(2)}) async-start(), calls=%async_computation.4 | async-start | bytes 1671168 | tf_op jit(solution)/shard_map/all_gather | solution.py:54
  248.9 137.1 %copy-start.2 = (bf16[2,576,1024]{2,0,1:T(2,128)(2,1)}, bf16[2,576,1024]{2,0,1:T(2,128)(2,1)S(1)}, u32[]{:S(2)}) copy-start(bf16[2,576,1024]{2,0,1:T(2,128)(2,1)S(1)} %get-tuple-element.20) | copy-start | bytes 7077892
  385.9 3.9 copy-start.4
  395.2 72.3 %all-to-all-start.2 = ((bf16[2,32,18,1024]{3,0,2,1:T(2,128)(2,1)}), bf16[2,32,18,1024]{3,0,2,1:T(2,128)(2,1)S(1)}, u32[]{:S(2)}, u32[]{:S(2)}) async-start(bf16[2,32,18,1024]{3,0,2,1:T(2,128)(2,1)} %bitcast.5), calls=%async_computation.2 | async-start | bytes 4718592 | tf_op jit(solution)/shard_map/all_to_all | solution.py:68
  467.5 1.4 copy-start
  468.8 249.1 %all-to-all-start.3 = ((bf16[2,32,18,1024]{3,0,2,1:T(2,128)(2,1)}), bf16[2,32,18,1024]{3,0,2,1:T(2,128)(2,1)}, u32[]{:S(2)}, u32[]{:S(2)}) async-start(bf16[2,32,18,1024]{3,0,2,1:T(2,128)(2,1)} %bitcast.7), calls=%async_computation.3 | async-start | bytes 4718592 | tf_op jit(solution)/shard_map/all_to_all | solution.py:71
  487.1 3.5 copy-start.3
  487.1 213.9 %all-reduce.3.cloned.1.call-start = ((), (), s32[]{:S(2)}) async-start(), calls=%async_computation.6 | async-start | bytes 6291456
  487.2 3.4 copy-start.8
  498.6 204.8 %copy-start.1 = (bf16[2,32,18,1024]{3,0,2,1:T(2,128)(2,1)S(1)}, bf16[2,32,18,1024]{3,0,2,1:T(2,128)(2,1)}, u32[]{:S(2)}) copy-start(bf16[2,32,18,1024]{3,0,2,1:T(2,128)(2,1)} %copy-done) | copy-start | bytes 7077892
Sparse Core Ops, SparseCore 0:
  100.7 180.7 all-gather.4
  283.6 102.3 all-gather.2
  498.8 202.2 all-reduce.2
where the time goes:
time: 746 us; the launch traced here: 741 us
  waiting for transfers between devices  528 us (71%)
  local copies, waits for them, and re-layouts  88.7 us (12%)
  starting transfers between devices  58.8 us (8%)
  other arithmetic  28.3 us (4%)
  matrix products  21.4 us (3%)
  between operations  14.9 us (2%)
    unnamed x4, waiting for transfers between devices  202 us
    all_to_all x1, waiting for transfers between devices, per_device(): lax.all_to_all(send_pair.reshape(exp_local, ctx_count, capacity, 2 * widt...  142 us
    all_gather x1, waiting for transfers between devices, per_device(): lax.all_gather(w_down, 'dp', axis=2, tiled=True)  99.7 us
    all_to_all x1, waiting for transfers between devices, per_device(): lax.all_to_all(grad_rows.reshape(block_shape), 'ctx', split_axis=1, conca...  52.4 us
    all_gather x1, waiting for transfers between devices, per_device(): lax.all_gather(w_up, 'dp', axis=1, tiled=True)  32.6 us
    all_to_all x1, starting transfers between devices, per_device(): lax.all_to_all(outputs.reshape(block_shape), 'ctx', split_axis=1, concat_...  18.3 us
    another operation x3, other arithmetic  18.2 us
    all_to_all x1, starting transfers between devices, per_device(): lax.all_to_all(send_gate.reshape(slot_shape), 'ctx', split_axis=1, concat...  15.4 us
  transfers between devices with their start and end apart: 7, of which 5 were waited for; matrix products, arithmetic and copies ran while one was open for 11% of the time, Pallas kernels for 0%

commit v1 on v0

--- a/solution.py
+++ b/solution.py
@@ -2,6 +2,11 @@
 import jax.numpy as jnp
 from jax import lax
 from jax.sharding import PartitionSpec as P
+
+
+def swapped_in(x, name, along):
+    repeated = jnp.stack([x] * lax.axis_size(name))
+    return jnp.concatenate(lax.all_to_all(repeated, name, 0, 0), axis=along)
 
 
 def swish_grad(pre_act, sigmoid_a):
@@ -51,7 +56,7 @@
     rows_gate = recv_gate.reshape(exp_local, row_len)
     up_full, down_full = (
         lax.all_gather(w_up, "dp", axis=1, tiled=True),
-        lax.all_gather(w_down, "dp", axis=2, tiled=True),
+        swapped_in(w_down, "dp", 2),
     )
     pre_act = jnp.einsum("erd,edf->erf", rows_x, up_full, preferred_element_type=jnp.float32)
     sigmoid_a = jax.nn.sigmoid(pre_act)

time: 746 us -> 680 us (0.912)
  waiting for transfers between devices: 528 us -> 430 us
  blocking collectives: 0 us -> 26.2 us
    all_gather x1 -> x0, waiting for transfers between devices: 99.7 us -> none  [per_device(): lax.all_gather(w_down, 'dp', axis=2, tiled=True)]
    all_to_all x0 -> x1, blocking collectives: none -> 26.2 us  [per_device(): lax.all_to_all(send_gate.reshape(slot_shape), 'ctx', split_axis=1, concat...]
    all_to_all x1, starting transfers between devices: 12.6 us -> 31.8 us  [per_device(): lax.all_to_all(grad_rows.reshape(block_shape), 'ctx', split_axis=1, conca...]
    all_to_all x1, starting transfers between devices: 15.4 us -> 4.75 us  [swapped_in(): return jnp.concatenate(lax.all_to_all(repeated, name, 0, 0), axis=along)]
    unnamed x4 -> x3, waiting for transfers between devices: 202 us -> 199 us
  transfers between devices with their start and end apart: 7 -> 6, of which waited for: 5 -> 4; matrix products, arithmetic and copies ran while one was open for 11% -> 12% of each run, Pallas kernels for 0% -> 0%
where the time goes in v1:
time: 680 us; the launch traced here: 674 us
  waiting for transfers between devices  430 us (63%)
  local copies, waits for them, and re-layouts  90.7 us (13%)
  starting transfers between devices  65 us (10%)
  other arithmetic  28.4 us (4%)
  blocking collectives  26.2 us (4%)
  matrix products  18.4 us (3%)
  between operations  15.3 us (2%)
    unnamed x3, waiting for transfers between devices  199 us
    all_to_all x1, waiting for transfers between devices, per_device(): lax.all_to_all(send_pair.reshape(exp_local, ctx_count, capacity, 2 * widt...  148 us
    all_to_all x1, waiting for transfers between devices, per_device(): lax.all_to_all(grad_rows.reshape(block_shape), 'ctx', split_axis=1, conca...  53.1 us
    all_to_all x1, starting transfers between devices, per_device(): lax.all_to_all(grad_rows.reshape(block_shape), 'ctx', split_axis=1, conca...  31.8 us
    all_gather x1, waiting for transfers between devices, per_device(): lax.all_gather(w_up, 'dp', axis=1, tiled=True)  30.7 us
    all_to_all x1, blocking collectives, per_device(): lax.all_to_all(send_gate.reshape(slot_shape), 'ctx', split_axis=1, concat...  26.2 us
    all_to_all x1, starting transfers between devices, per_device(): lax.all_to_all(outputs.reshape(block_shape), 'ctx', split_axis=1, concat_...  22.3 us
    another operation x3, other arithmetic  18.2 us
  transfers between devices with their start and end apart: 6, of which 4 were waited for; matrix products, arithmetic and copies ran while one was open for 12% of the time, Pallas kernels for 0%

profile of v1, /device:TPU:64, one launch (start us, length us, event | category | flops | bytes accessed | tf_op | source)
XLA Modules:
  0.0 674.3 jit_solution(4106499183241357686)
XLA Ops:
  7.2 0.8 copy.58
  8.3 18.0 %reduce-window.6 = s32[64,8,128]{2,1,0:T(8,128)S(1)} reduce-window(s32[64,8,128]{2,1,0:T(8,128)S(1)} %fusion.20, s32[]{:T(128)} %constant.60.clone.1), window={size=1x1x128 pad=0_0x0_0x127_0}, to_apply=%region_0.0 | reduce-window | flops 8323072 | bytes 524292 | tf_op jit(solution)/shard_map/reduce-window
  27.2 7.6 %scatter_custom_fusion = bf16[1152]{0:T(1024)(128)(2,1)S(1)} fusion(s32[1024]{0:T(1024)S(1)} %bitcast.64, bf16[1024]{0:T(1024)(128)(2,1)S(1)} %reshape.248, bf16[]{:T(256)} %constant.59.clone.1), kind=kCustom, calls=%fused_computation.60 | custom fusion | bytes 2306 | tf_op jit(solution)/shard_map/scatter | solution.py:37
  35.0 26.2 %all_to_all.25 = bf16[2,32,18]{2,0,1:T(2,128)(2,1)S(1)} all-to-all(bf16[2,32,18]{2,0,1:T(2,128)(2,1)S(1)} %copy.64), channel_id=1, replica_groups=mesh['dp'=16,'ctx'=32] {'ctx'}, dimensions={1} | all-to-all | bytes 4608 | tf_op jit(solution)/shard_map/all_to_all | solution.py:48
  61.2 1.4 stack.11
  62.6 4.7 all-to-all-start.2
  67.3 4.8 scatter_custom_fusion.1
  72.2 5.9 gather_fusion
  78.1 7.5 %gather.13 = bf16[2,32,18,2048]{3,2,1,0:T(8,128)(2,1)} reshape(bf16[1152,2048]{1,0:T(8,128)(2,1)} %gather_fusion) | data formatting | bytes 9437184 | tf_op jit(solution)/shard_map/jit(_take)/gather | solution.py:36
  85.6 0.1 broadcast_in_dim.27
  85.8 6.0 broadcast_select_fusion
  91.8 9.8 %copy.67 = bf16[2,32,18,2048]{3,0,2,1:T(2,128)(2,1)} copy(bf16[2,32,18,2048]{3,2,1,0:T(8,128)(2,1)} %broadcast_select_fusion) | data formatting | bytes 9437184 | tf_op jit(solution)/shard_map/jit(_take)/select_n | solution.py:36
  101.6 5.9 all-to-all-start.1
  107.5 0.2 all-gather.2.cloned.1.call-start
  107.7 0.5 all-gather.2.cloned.1.call-update
  108.6 1.3 copy.69
  109.9 148.1 %all-to-all-done.1 = bf16[2,32,18,2048]{3,0,2,1:T(2,128)(2,1)} async-done(((bf16[2,32,18,2048]{3,0,2,1:T(2,128)(2,1)}), bf16[2,32,18,2048]{3,0,2,1:T(2,128)(2,1)}, u32[]{:S(2)}, u32[]{:S(2)}) %all-to-all-start.1) | async-done | bytes 4718624 | tf_op jit(solution)/shard_map/all_to_all | solution.py:41
  258.0 7.0 %fusion.30 = (bf16[2,576,1024]{2,0,1:T(2,128)(2,1)S(1)}, bf16[2,576,1024]{2,0,1:T(2,128)(2,1)}) fusion(bf16[2,576,2048]{2,0,1:T(2,128)(2,1)} %bitcast.4), kind=kLoop, calls=%fused_computation.62 | loop fusion | bytes 9437184 | tf_op jit(solution)/shard_map/slice | solution.py:55
  265.0 30.7 %all-gather.2.cloned.1.call-done = bf16[2,1024,384]{2,1,0:T(8,128)(2,1)} async-done(((bf16[2,64,384]{2,1,0:T(8,128)(2,1)}), bf16[2,1024,384]{2,1,0:T(8,128)(2,1)}) %all-gather.2.cloned.1.call-update) | async-done | bytes 1572880 | tf_op jit(solution)/shard_map/all_gather | solution.py:58
  295.8 3.6 fusion.4
  299.4 1.9 multiply_convert_fusion.4
  301.3 0.2 copy-done.5
  301.5 1.4 convolution_convert_fusion.1
  302.9 3.8 copy.72
  306.7 31.8 %all-to-all-start.3 = ((bf16[2,32,18,1024]{3,0,2,1:T(2,128)(2,1)}), bf16[2,32,18,1024]{3,0,2,1:T(2,128)(2,1)S(1)}, u32[]{:S(2)}, u32[]{:S(2)}) async-start(bf16[2,32,18,1024]{3,0,2,1:T(2,128)(2,1)} %bitcast.7), calls=%async_computation.3 | async-start | bytes 4718592 | tf_op jit(solution)/shard_map/all_to_all | solution.py:73
  338.6 3.4 convolution_convert_fusion
  341.9 3.8 copy.75
  345.8 53.1 %all-to-all-done.3 = bf16[2,32,18,1024]{3,0,2,1:T(2,128)(2,1)S(1)} async-done(((bf16[2,32,18,1024]{3,0,2,1:T(2,128)(2,1)}), bf16[2,32,18,1024]{3,0,2,1:T(2,128)(2,1)S(1)}, u32[]{:S(2)}, u32[]{:S(2)}) %all-to-all-start.3) | async-done | bytes 2359328 | tf_op jit(solution)/shard_map/all_to_all | solution.py:73
  398.9 1.5 copy-done
  400.4 22.3 %all-to-all-start.4 = ((bf16[2,32,18,1024]{3,0,2,1:T(2,128)(2,1)}), bf16[2,32,18,1024]{3,0,2,1:T(2,128)(2,1)}, u32[]{:S(2)}, u32[]{:S(2)}) async-start(bf16[2,32,18,1024]{3,0,2,1:T(2,128)(2,1)} %bitcast.10), calls=%async_computation.4 | async-start | bytes 4718592 | tf_op jit(solution)/shard_map/all_to_all | solution.py:76
  422.8 3.4 fusion.12
  426.2 1.8 fusion.15
  428.0 0.3 pad_maximum_fusion
  428.3 5.9 copy.78
  434.3 1.4 dynamic-slice
  436.4 198.0 %all-reduce.3.cloned.1.call-done = bf16[1024,2,2,384]{3,2,1,0:T(2,128)(2,1)} async-done(((bf16[1024,2,2,384]{3,2,1,0:T(2,128)(2,1)}), bf16[1024,2,2,384]{3,2,1,0:T(2,128)(2,1)}) %all-reduce.3.cloned.1.call-update) | async-done | bytes 3145744
  634.3 1.1 dynamic-slice_bitcast_fusion
  635.4 0.7 copy.79
  636.1 0.7 copy.80
  636.7 2.5 copy.73
  639.2 2.9 reshape.214
  642.2 5.4 gather_fusion.1
  647.6 3.7 bitcast_reduce_fusion
  651.3 4.2 copy.76
  655.5 2.9 reshape.217
  658.4 5.4 gather_fusion.2
  663.8 2.8 fusion
  666.6 0.7 copy.84
  (51 shorter events, 1.8 us)
Async XLA Ops:
  7.2 19.7 %copy-start.9 = (bf16[128,8]{0,1:T(8,128)(2,1)S(1)}, bf16[128,8]{0,1:T(8,128)(2,1)}, u32[]{:S(2)}) copy-start(bf16[128,8]{0,1:T(8,128)(2,1)} %param.8) | copy-start | bytes 6148
  7.2 54.0 %copy-start.8 = (bf16[2,384,64]{1,2,0:T(8,128)(2,1)S(1)}, bf16[2,384,64]{1,2,0:T(8,128)(2,1)}, u32[]{:S(2)}) copy-start(bf16[2,384,64]{1,2,0:T(8,128)(2,1)} %param.11) | copy-start | bytes 294916
  61.2 11.0 %copy-start.6 = (bf16[128,1024]{1,0:T(8,128)(2,1)S(1)}, bf16[128,1024]{1,0:T(8,128)(2,1)}, u32[]{:S(2)}) copy-start(bf16[128,1024]{1,0:T(8,128)(2,1)} %param.6) | copy-start | bytes 786436
  61.2 11.0 %copy-start.7 = (bf16[128,1024]{1,0:T(8,128)(2,1)S(1)}, bf16[128,1024]{1,0:T(8,128)(2,1)}, u32[]{:S(2)}) copy-start(bf16[128,1024]{1,0:T(8,128)(2,1)} %param.7) | copy-start | bytes 786436
  62.6 39.0 %all-to-all-start.2 = ((bf16[16,2,384,64]{2,3,1,0:T(8,128)(2,1)}), bf16[16,2,384,64]{2,3,1,0:T(8,128)(2,1)S(1)}, u32[]{:S(2)}, u32[]{:S(2)}) async-start(bf16[16,2,384,64]{2,3,1,0:T(8,128)(2,1)} %stack.11), calls=%async_computation.2 | async-start | bytes 3145728 | tf_op jit(solution)/shard_map/all_to_all | solution.py:9
  101.6 156.4 %all-to-all-start.1 = ((bf16[2,32,18,2048]{3,0,2,1:T(2,128)(2,1)}), bf16[2,32,18,2048]{3,0,2,1:T(2,128)(2,1)}, u32[]{:S(2)}, u32[]{:S(2)}) async-start(bf16[2,32,18,2048]{3,0,2,1:T(2,128)(2,1)} %copy.67), calls=%async_computation.1 | async-start | bytes 9437184 | tf_op jit(solution)/shard_map/all_to_all | solution.py:41
  107.5 188.3 %all-gather.2.cloned.1.call-start = ((), (), s32[]{:S(2)}) async-start(), calls=%async_computation.5 | async-start | bytes 1671168 | tf_op jit(solution)/shard_map/all_gather | solution.py:58
  265.0 34.4 %copy-start.2 = (bf16[2,576,1024]{2,0,1:T(2,128)(2,1)}, bf16[2,576,1024]{2,0,1:T(2,128)(2,1)S(1)}, u32[]{:S(2)}) copy-start(bf16[2,576,1024]{2,0,1:T(2,128)(2,1)S(1)} %get-tuple-element.20) | copy-start | bytes 7077892
  295.8 3.7 copy-start.4
  299.4 1.9 copy-start.10
  299.4 2.0 copy-start.5
  306.7 92.2 %all-to-all-start.3 = ((bf16[2,32,18,1024]{3,0,2,1:T(2,128)(2,1)}), bf16[2,32,18,1024]{3,0,2,1:T(2,128)(2,1)S(1)}, u32[]{:S(2)}, u32[]{:S(2)}) async-start(bf16[2,32,18,1024]{3,0,2,1:T(2,128)(2,1)} %bitcast.7), calls=%async_computation.3 | async-start | bytes 4718592 | tf_op jit(solution)/shard_map/all_to_all | solution.py:73
  398.9 1.5 copy-start
  400.4 250.9 %all-to-all-start.4 = ((bf16[2,32,18,1024]{3,0,2,1:T(2,128)(2,1)}), bf16[2,32,18,1024]{3,0,2,1:T(2,128)(2,1)}, u32[]{:S(2)}, u32[]{:S(2)}) async-start(bf16[2,32,18,1024]{3,0,2,1:T(2,128)(2,1)} %bitcast.10), calls=%async_computation.4 | async-start | bytes 4718592 | tf_op jit(solution)/shard_map/all_to_all | solution.py:76
  422.7 3.5 copy-start.3
  422.7 211.6 %all-reduce.3.cloned.1.call-start = ((), (), s32[]{:S(2)}) async-start(), calls=%async_computation.6 | async-start | bytes 6291456
  422.7 3.4 copy-start.11
  434.2 202.5 %copy-start.1 = (bf16[2,32,18,1024]{3,0,2,1:T(2,128)(2,1)S(1)}, bf16[2,32,18,1024]{3,0,2,1:T(2,128)(2,1)}, u32[]{:S(2)}) copy-start(bf16[2,32,18,1024]{3,0,2,1:T(2,128)(2,1)} %copy-done) | copy-start | bytes 7077892
Sparse Core Ops, SparseCore 0:
  110.4 185.2 all-gather.1
  434.4 199.9 all-reduce.2
